TPU v7x, 256 devices: a whole 4x4x8 slice. The times are simulated.
256 devices in a mesh: rows: 16 (over z, core), blk: 16 (over x, y).
Axes of the slice: x: 4, y: 4, z: 8, core: 2. Of those that a mesh axis runs over, the one named last changes fastest.
Arguments:
- jacobian: float32 [65536, 4096], P('rows', 'blk'), may hold values from -6 to 6
- row_weight: float32 [65536], P('rows'), may hold values from 0.3 to 3
- col_scale: float32 [4096], P('blk'), may hold values from 0.3 to 3
- round_count: int32 [2], replicated, may hold values from 12 to 24, as said below
- move_flag: int32 [2, 16], P(None, 'blk'), may hold values 0 or 1
Outputs:
- rotated: float32 [65536, 4096], P('rows', 'blk')
- orth_basis: float32 [4096, 4096], P('rows', 'blk')
Inputs may be any that keep to these rules, and one draw needn't show every extreme that they name: `round_count`: one entry equals 24.
All inputs are finite; a program needn't handle non-finite values. No bound on the sum of `move_flag` on one device may be relied on, other than what follows from the above.
Results may differ from a plain program's by a relative error of at most 0.0004.
Values sent between devices are 32-bit elements; how exact they have to be, the bound alone decides.
A program may use at most 64 MiB of HBM per device.

v0:
```python
import jax
import jax.numpy as jnp
from jax import lax
from jax.experimental import pallas as pl
from jax.experimental.pallas import tpu as pltpu
from jax.sharding import PartitionSpec as P

MESH = pl.DeviceIdType.MESH
B = 128
ROUNDS = 24
CH = 256
F32 = jnp.float32
BF16 = jnp.bfloat16


def split(x):
    high = x.astype(BF16)
    return high, (x - high.astype(F32)).astype(BF16)


def rotation(first, second, cross, live):
    diff = second - first
    radius = jnp.sqrt(diff * diff + 4.0 * cross * cross)
    signs = jnp.where(diff >= 0.0, 1.0, -1.0)
    tangent = signs * 2.0 * cross / (jnp.abs(diff) + radius)
    cosine = 1.0 / jnp.sqrt(1.0 + tangent * tangent)
    sine = cosine * tangent
    return jnp.where(live, cosine, 1.0), jnp.where(live, sine, 0.0)


def tile(k):
    return pl.ds(8 * k, 8)


def spaced(k, start=0):
    return pl.ds(start + k, 8, stride=16)


def inner_rounds(count, gram, q, a, c, e, d, ccol, scol):
    count = jnp.full((8, B), count, jnp.int32)
    lane = lax.broadcasted_iota(jnp.int32, (8, B), 1)
    sub = lax.broadcasted_iota(jnp.int32, (8, B), 0)
    low = lane % 16
    on_diag = (lane // 16) == sub
    nxt = (lane + (B - 1)) % B
    nlow = nxt % 16
    on_next = (nxt // 16) == sub
    ccol[...] = jnp.transpose(gram[B : 2 * B, :])
    for k in range(16):
        a[tile(k), :] = gram[spaced(k), :]
        c[tile(k), :] = gram[spaced(k, B), :]
        e[tile(k), :] = ccol[spaced(k), :]
        d[tile(k), :] = gram[spaced(k, 2 * B), :]
    rows = lax.broadcasted_iota(jnp.int32, (2 * B, 2 * B), 0)
    cols = lax.broadcasted_iota(jnp.int32, (2 * B, 2 * B), 1)
    q[...] = (rows == cols).astype(F32)

    def pick(ref):
        acc = jnp.zeros((8, B), F32)
        for k in range(16):
            acc = jnp.where(low == k, ref[tile(k), :], acc)
        return total(jnp.where(on_diag, acc, 0.0))

    def total(x):
        return jnp.broadcast_to(jnp.sum(x, axis=0, keepdims=True), (8, B))

    def spread(cs, sn):
        ccol[...] = jnp.transpose(jnp.broadcast_to(cs[0:1], (B, B)))
        scol[...] = jnp.transpose(jnp.broadcast_to(sn[0:1], (B, B)))

    cs, sn = rotation(pick(a), pick(d), pick(c), 0 < count)
    spread(cs, sn)

    def one(index, carry):
        cs, sn = carry
        acc_a = acc_c = acc_d = jnp.zeros((8, B), F32)
        first = None
        for k in range(16):
            before = tile((k - 1) % 16)
            ck, sk = ccol[spaced(k), :], scol[spaced(k), :]
            ak, bk, ek, dk = a[tile(k), :], c[tile(k), :], e[tile(k), :], d[tile(k), :]
            a1 = ck * ak - sk * ek
            e1 = sk * ak + ck * ek
            b1 = ck * bk - sk * dk
            d1 = sk * bk + ck * dk
            a2 = a1 * cs - b1 * sn
            b2 = a1 * sn + b1 * cs
            e2 = e1 * cs - d1 * sn
            d2 = e1 * sn + d1 * cs
            acc_a = jnp.where(low == k, a2, acc_a)
            acc_d = jnp.where(low == k, d2, acc_d)
            acc_c = jnp.where(nlow == k, b2, acc_c)
            a[tile(k), :] = a2
            c[tile(k), :] = pltpu.roll(b2, B - 1, 1)
            d3 = pltpu.roll(d2, B - 1, 1)
            if k == 0:
                first = (e2, d3)
            else:
                e[before, :] = e2
                d[before, :] = d3
        e[tile(15), :] = pltpu.roll(first[0], 7, 0)
        d[tile(15), :] = pltpu.roll(first[1], 7, 0)
        diag_a = total(jnp.where(on_diag, acc_a, 0.0))
        diag_d = pltpu.roll(total(jnp.where(on_diag, acc_d, 0.0)), B - 1, 1)
        diag_c = pltpu.roll(total(jnp.where(on_next, acc_c, 0.0)), B - 1, 1)
        new = rotation(diag_a, diag_d, diag_c, index + 1 < count)
        for k in range(32):
            qa, qb = q[tile(k), 0:B], q[tile(k), B : 2 * B]
            q[tile(k), 0:B] = qa * cs - qb * sn
            q[tile(k), B : 2 * B] = pltpu.roll(qa * sn + qb * cs, B - 1, 1)
        spread(*new)
        return new

    lax.fori_loop(0, ROUNDS, one, (cs, sn))
    extra = ROUNDS - count
    for k in range(32):
        qb = q[tile(k), B : 2 * B]
        for bit in range(5):
            qb = jnp.where((extra >> bit) % 2 == 1, pltpu.roll(qb, 1 << bit, 1), qb)
        q[tile(k), B : 2 * B] = qb


def body(
    counts, flags, x_hbm, out_hbm, w_out,
    x, s, t, tin, u, g, hh, hl, q, qhi, qlo, ra, rc, re, rd, ccol, scol, half, piece, full, w1, w1in, w2, w2in,
    load_sem, store_sem, t_send, t_recv, u_send, u_recv, core_send, core_recv, z_send, z_recv, w_send, w_recv,
):
    row, blk = lax.axis_index("rows"), lax.axis_index("blk")
    n_blk = lax.axis_size("blk")
    z, core = row // 2, row % 2
    chunks = x.shape[0] // CH
    fwd = (row, (blk + 1) % n_blk)
    bwd = (row, (blk + n_blk - 1) % n_blk)
    twin = (row + 1 - 2 * core, blk)
    peers = [(((z + i) % 8) * 2 + core, blk) for i in range(1, 8)]
    owner = row == blk
    next_owner = row == (blk + n_blk - 1) % n_blk
    third_owner = row == (blk + n_blk - 2) % n_blk

    def at(c):
        return pl.ds(pl.multiple_of(c * CH, CH), CH)

    def load(c):
        return pltpu.make_async_copy(x_hbm.at[at(c), :], x.at[at(c), :], load_sem.at[c])

    lax.fori_loop(0, chunks, lambda c, _: (load(c).start(), 0)[1], 0)

    barrier = pltpu.get_barrier_semaphore()
    for device in [bwd, twin] + peers:
        pl.semaphore_signal(barrier, inc=1, device_id=device, device_id_type=MESH)
    pl.semaphore_wait(barrier, 9)

    def remote(src, dst, send, recv, device):
        return pltpu.make_async_remote_copy(
            src_ref=src, dst_ref=dst, send_sem=send, recv_sem=recv, device_id=device, device_id_type=MESH
        )

    def add_gram(block, first):
        high, low = split(block)
        dims = (((0,), (0,)), ((), ()))
        both = lax.dot_general(high, jnp.concatenate([high, low], 1), dims, preferred_element_type=F32)
        small = low.astype(F32)
        small = jnp.sum((small * small).reshape(CH // 8, 8, 2 * B), axis=0)
        hh[...] = hh[...] + both[:, : 2 * B]
        hl[...] = hl[...] + both[:, 2 * B :]
        return small

    def gram(get):
        hh[...] = jnp.zeros_like(hh)
        hl[...] = jnp.zeros_like(hl)
        small = lax.fori_loop(
            0, chunks, lambda c, acc: acc + add_gram(get(c), c), jnp.zeros((8, 2 * B), F32)
        )
        small = jnp.sum(small, axis=0, keepdims=True)
        rows = lax.broadcasted_iota(jnp.int32, (B, B), 0)
        cols = lax.broadcasted_iota(jnp.int32, (B, B), 1)
        for place, (i, j) in enumerate(((0, 0), (0, 1), (1, 1))):
            here, there = pl.ds(i * B, B), pl.ds(j * B, B)
            block = hh[here, there] + (hl[here, there] + jnp.transpose(hl[there, here]))
            if i == j:
                block = block + jnp.where(rows == cols, small[:, i * B : (i + 1) * B], 0.0)
            g[pl.ds(place * B, B), :] = block

    def reduce_all(step):
        mine = pl.ds(pl.multiple_of(core * 192, 8), 192)
        other = pl.ds(pl.multiple_of((1 - core) * 192, 8), 192)
        copy = remote(g.at[other, :], half.at[:, :], core_send.at[2 * step], core_recv.at[2 * step], twin)
        copy.start()
        copy.wait()
        g[mine, :] = g[mine, :] + half[...]
        copies = []
        for i, peer in enumerate(peers):
            rows = pl.ds(pl.multiple_of(core * 192 + (peer[0] // 2) * 24, 8), 24)
            copies.append(remote(
                g.at[rows, :], piece.at[step, i], z_send.at[step, i], z_recv.at[step, i], peer
            ))
            copies[-1].start()
        for copy in copies:
            copy.wait()
        own = pl.ds(pl.multiple_of(core * 192 + z * 24, 8), 24)
        total = g[own, :]
        for i in range(7):
            total = total + piece[step, i]
        done = full.at[step]
        done[own, :] = total
        copies = []
        for i, peer in enumerate(peers):
            copies.append(remote(
                done.at[own, :], done.at[own, :], z_send.at[step, 7 + i], z_recv.at[step, 7 + i], peer
            ))
            copies[-1].start()
        for copy in copies:
            copy.wait()
        copy = remote(done.at[mine, :], done.at[mine, :], core_send.at[2 * step + 1], core_recv.at[2 * step + 1], twin)
        copy.start()
        copy.wait()

    def solve(step):
        reduce_all(step)
        inner_rounds(counts[step], full.at[step], q, ra, rc, re, rd, ccol, scol)
        left = jnp.full((8, B), flags[step, 0], jnp.int32) == 1
        for k in range(32):
            qa, qb = q[tile(k), 0:B], q[tile(k), B : 2 * B]
            q[tile(k), 0:B] = jnp.where(left, qb, qa)
            q[tile(k), B : 2 * B] = jnp.where(left, qa, qb)
        qhi[...], qlo[...] = split(q[...])

    def multiply(block):
        high, low = split(block)
        qh = qhi[...]
        out = jnp.dot(low, qh, preferred_element_type=F32)
        out = out + jnp.dot(high, qlo[...], preferred_element_type=F32)
        return out + jnp.dot(high, qh, preferred_element_type=F32)

    def t_copy(c):
        return remote(t.at[at(c), :], tin.at[at(c), :], t_send.at[c], t_recv.at[c], fwd)

    def u_copy(c):
        return remote(u.at[at(c), :], out_hbm.at[at(c), B : 2 * B], u_send.at[c], u_recv.at[c], fwd)

    def w_copy(step):
        if step == 0:
            return remote(w1.at[:, B : 2 * B], w1in, w_send.at[0], w_recv.at[0], fwd)
        return remote(w2.at[:, B : 2 * B], w2in, w_send.at[1], w_recv.at[1], fwd)

    def loaded(c):
        load(c).wait()
        return x[at(c), :]

    gram(loaded)
    solve(0)

    def first_step(c, _):
        y = multiply(x[at(c), :])
        s[at(c), :] = y[:, :B]
        t[at(c), :] = y[:, B:]
        t_copy(c).start()
        return 0

    lax.fori_loop(0, chunks, first_step, 0)
    @pl.when(owner)
    def _():
        w1[...] = q[...]
        w_copy(0).start()

    @pl.when(jnp.logical_not(owner))
    def _():
        w1[...] = jnp.zeros_like(w1)

    @pl.when(jnp.logical_not(next_owner))
    def _():
        w1in[...] = jnp.zeros_like(w1in)

    def pair(c):
        return jnp.concatenate([s[at(c), :], tin[at(c), :]], 1)

    def arrived(c):
        t_copy(c).wait_recv()
        return pair(c)

    gram(arrived)
    solve(1)

    def stay_copy(c):
        return pltpu.make_async_copy(s.at[at(c), :], out_hbm.at[at(c), 0:B], store_sem.at[c])

    def second_step(c, _):
        y = multiply(pair(c))
        u[at(c), :] = y[:, B:]
        u_copy(c).start()
        s[at(c), :] = y[:, :B]
        stay_copy(c).start()
        return 0

    lax.fori_loop(0, chunks, second_step, 0)

    @pl.when(next_owner)
    def _():
        w_copy(0).wait_recv()

    w2[...] = multiply(jnp.concatenate([w1[:, :B], w1in[...]], 1))
    w_out[:, :B] = w2[:, :B]

    @pl.when(jnp.logical_or(owner, next_owner))
    def _():
        w_copy(1).start()

    @pl.when(jnp.logical_not(jnp.logical_or(next_owner, third_owner)))
    def _():
        w_out[:, B:] = jnp.zeros((2 * B, B), F32)

    def finish(c, _):
        t_copy(c).wait_send()
        u_copy(c).wait_send()
        u_copy(c).wait_recv()
        stay_copy(c).wait()
        return 0

    lax.fori_loop(0, chunks, finish, 0)

    @pl.when(owner)
    def _():
        w_copy(0).wait_send()

    @pl.when(jnp.logical_or(owner, next_owner))
    def _():
        w_copy(1).wait_send()

    @pl.when(jnp.logical_or(next_owner, third_owner))
    def _():
        w_copy(1).wait_recv()
        w_out[:, B:] = w2in[...]


def per_device(jacobian, row_weight, col_scale, round_count, move_flag):
    scaled = jacobian * row_weight[:, None] * col_scale[None, :]
    rows = scaled.shape[0]
    chunks = rows // CH
    anywhere = pl.BlockSpec(memory_space=pl.ANY)
    vmem = pl.BlockSpec(memory_space=pltpu.VMEM)
    smem = pl.BlockSpec(memory_space=pltpu.SMEM)
    dma = pltpu.SemaphoreType.DMA
    square = pltpu.VMEM((B, B), F32)
    wide = pltpu.VMEM((2 * B, 2 * B), F32)
    tall = pltpu.VMEM((2 * B, B), F32)
    column = pltpu.VMEM((rows, B), F32)
    return pl.pallas_call(
        body,
        out_shape=(
            jax.ShapeDtypeStruct((rows, 2 * B), F32),
            jax.ShapeDtypeStruct((2 * B, 2 * B), F32),
        ),
        in_specs=[smem, smem, anywhere],
        out_specs=(anywhere, vmem),
        scratch_shapes=[
            pltpu.VMEM((rows, 2 * B), F32), column, column, column, column,
            pltpu.VMEM((3 * B, B), F32), wide, wide, wide,
            pltpu.VMEM((2 * B, 2 * B), BF16), pltpu.VMEM((2 * B, 2 * B), BF16),
            square, square, square, square, square, square,
            pltpu.VMEM((192, B), F32), pltpu.VMEM((2, 7, 24, B), F32), pltpu.VMEM((2, 3 * B, B), F32),
            wide, tall, wide, tall,
            dma((chunks,)), dma((chunks,)), dma((chunks,)), dma((chunks,)), dma((chunks,)), dma((chunks,)),
            dma((4,)), dma((4,)), dma((2, 14)), dma((2, 14)), dma((2,)), dma((2,)),
        ],
        compiler_params=pltpu.CompilerParams(
            collective_id=0, has_side_effects=True, vmem_limit_bytes=56 * 2**20
        ),
        name="jacobi",
    )(round_count, move_flag, scaled)


def solution(mesh):
    in_specs = (P("rows", "blk"), P("rows"), P("blk"), P(), P(None, "blk"))
    out_specs = (P("rows", "blk"), P("rows", "blk"))
    return jax.shard_map(
        per_device, mesh=mesh, in_specs=in_specs, out_specs=out_specs, check_vma=False
    )
```

profile of v0, /device:TPU:1, one launch (start us, length us, event | category | flops | bytes accessed | tf_op | source)
XLA Modules:
  0.0 167.6 jit_solution(11429589419522735526)
XLA Ops:
  0.6 1.3 copy.7.flags
  1.9 3.9 %multiply_multiply_fusion.x_hbm = f32[4096,256]{1,0:T(8,128)} fusion(f32[4096,256]{1,0:T(8,128)} %param.5, f32[256]{0:T(256)} %param.7, f32[4096]{0:T(1024)} %param.6), kind=kLoop, calls=%fused_computation | loop fusion | flops 2097152 | bytes 8406016 | tf_op jit(solution)/shard_map/mul | solution.py:336
  5.9 156.5 %jacobi.1 = (f32[4096,256]{1,0:T(8,128)}, f32[256,256]{1,0:T(8,128)}) custom-call(s32[2]{0:T(128)} %counts.1, s32[2,1]{1,0:T(2,128)} %copy.7.flags, f32[4096,256]{1,0:T(8,128)} %multiply_multiply_fusion.x_hbm), custom_call_target="tpu_custom_call" | custom-call | tf_op jit(solution)/shard_map/jacobi/pallas_call | solution.py:347
  162.4 0.0 copy-start
  162.4 4.5 %copy.10 = f32[4096,256]{1,0:T(8,128)} copy(f32[4096,256]{1,0:T(8,128)} %get-tuple-element.4) | data formatting | bytes 8388608
  166.9 0.0 copy-done
  166.9 0.7 copy.11
Async XLA Ops:
  162.4 4.5 %copy-start = (f32[256,256]{1,0:T(8,128)S(1)}, f32[256,256]{1,0:T(8,128)}, u32[]{:S(2)}) copy-start(f32[256,256]{1,0:T(8,128)} %get-tuple-element.5) | copy-start | bytes 786436
where the time goes:
time: 169 us; the launch traced here: 168 us
  Pallas kernels  156 us (92%)
  local copies, waits for them, and re-layouts  6.52 us (4%)
  other arithmetic  3.94 us (2%)
    pallas_call x1, Pallas kernels, per_device(): pl.pallas_call(body, out_shape=(jax.ShapeDtypeStruct((rows, 2 * B), F32),...  156 us
    unnamed x5, local copies, waits for them, and re-layouts  6.52 us
    mul x1, other arithmetic, per_device(): scaled = jacobian * row_weight[:, None] * col_scale[None, :]  3.94 us

commit v1 on v0

--- a/solution.py
+++ b/solution.py
@@ -16,6 +16,11 @@
 def split(x):
     high = x.astype(BF16)
     return high, (x - high.astype(F32)).astype(BF16)
+
+
+def split_rest(x):
+    high = x.astype(BF16)
+    return high, x - high.astype(F32)
 
 
 def rotation(first, second, cross, live):
@@ -36,7 +41,7 @@
     return pl.ds(start + k, 8, stride=16)
 
 
-def inner_rounds(count, gram, q, a, c, e, d, ccol, scol):
+def inner_rounds(count, cross, q, a, c, e, d, ccol, scol):
     count = jnp.full((8, B), count, jnp.int32)
     lane = lax.broadcasted_iota(jnp.int32, (8, B), 1)
     sub = lax.broadcasted_iota(jnp.int32, (8, B), 0)
@@ -45,12 +50,10 @@
     nxt = (lane + (B - 1)) % B
     nlow = nxt % 16
     on_next = (nxt // 16) == sub
-    ccol[...] = jnp.transpose(gram[B : 2 * B, :])
+    ccol[...] = jnp.transpose(cross[...])
     for k in range(16):
-        a[tile(k), :] = gram[spaced(k), :]
-        c[tile(k), :] = gram[spaced(k, B), :]
+        c[tile(k), :] = cross[spaced(k), :]
         e[tile(k), :] = ccol[spaced(k), :]
-        d[tile(k), :] = gram[spaced(k, 2 * B), :]
     rows = lax.broadcasted_iota(jnp.int32, (2 * B, 2 * B), 0)
     cols = lax.broadcasted_iota(jnp.int32, (2 * B, 2 * B), 1)
     q[...] = (rows == cols).astype(F32)
@@ -113,28 +116,48 @@
 
     lax.fori_loop(0, ROUNDS, one, (cs, sn))
     extra = ROUNDS - count
+    surplus = [(extra >> bit) % 2 == 1 for bit in range(5)]
     for k in range(32):
         qb = q[tile(k), B : 2 * B]
         for bit in range(5):
-            qb = jnp.where((extra >> bit) % 2 == 1, pltpu.roll(qb, 1 << bit, 1), qb)
+            qb = jnp.where(surplus[bit], pltpu.roll(qb, 1 << bit, 1), qb)
         q[tile(k), B : 2 * B] = qb
+    return surplus
+
+
+def undo_moves(d, surplus):
+    tiles = [d[tile(k), :] for k in range(16)]
+    for bit in range(5):
+        move = 1 << bit
+        moved = []
+        for k in range(16):
+            value = pltpu.roll(tiles[(k - move) % 16], move, 1)
+            moved.append(value if k >= move else pltpu.roll(value, 1, 0))
+        tiles = [jnp.where(surplus[bit], new, old) for new, old in zip(moved, tiles)]
+    return tiles
 
 
 def body(
     counts, flags, x_hbm, out_hbm, w_out,
-    x, s, t, tin, u, g, hh, hl, q, qhi, qlo, ra, rc, re, rd, ccol, scol, half, piece, full, w1, w1in, w2, w2in,
-    load_sem, store_sem, t_send, t_recv, u_send, u_recv, core_send, core_recv, z_send, z_recv, w_send, w_recv,
+    x, s, t, tin, sin, u, v, g, hh, hl, q, qhi, qmid, qlo, ra, rc, re, rd, ccol, scol,
+    half, piece, full, cross, cross_half, own_piece, far_piece, cross_full, d_out, d_in, w1, w1in, w2, w2in,
+    load_sem, store_sem, t_send, t_recv, s_send, s_recv, u_send, u_recv,
+    core_send, core_recv, z_send, z_recv, far_send, far_recv, w_send, w_recv, d_send, d_recv,
 ):
     row, blk = lax.axis_index("rows"), lax.axis_index("blk")
     n_blk = lax.axis_size("blk")
     z, core = row // 2, row % 2
     chunks = x.shape[0] // CH
-    fwd = (row, (blk + 1) % n_blk)
-    bwd = (row, (blk + n_blk - 1) % n_blk)
+    mid = chunks // 2
+    next_blk = (blk + 1) % n_blk
+    last_blk = (blk + n_blk - 1) % n_blk
+    fwd, bwd = (row, next_blk), (row, last_blk)
     twin = (row + 1 - 2 * core, blk)
     peers = [(((z + i) % 8) * 2 + core, blk) for i in range(1, 8)]
+    far = [(((z + i) % 8) * 2 + core, next_blk) for i in range(8)]
+    far_from = [(((z + i) % 8) * 2 + core, last_blk) for i in range(8)]
     owner = row == blk
-    next_owner = row == (blk + n_blk - 1) % n_blk
+    next_owner = row == last_blk
     third_owner = row == (blk + n_blk - 2) % n_blk
 
     def at(c):
@@ -146,31 +169,30 @@
     lax.fori_loop(0, chunks, lambda c, _: (load(c).start(), 0)[1], 0)
 
     barrier = pltpu.get_barrier_semaphore()
-    for device in [bwd, twin] + peers:
+    for device in [twin, fwd] + peers + far_from:
         pl.semaphore_signal(barrier, inc=1, device_id=device, device_id_type=MESH)
-    pl.semaphore_wait(barrier, 9)
 
     def remote(src, dst, send, recv, device):
         return pltpu.make_async_remote_copy(
             src_ref=src, dst_ref=dst, send_sem=send, recv_sem=recv, device_id=device, device_id_type=MESH
         )
 
-    def add_gram(block, first):
-        high, low = split(block)
-        dims = (((0,), (0,)), ((), ()))
-        both = lax.dot_general(high, jnp.concatenate([high, low], 1), dims, preferred_element_type=F32)
-        small = low.astype(F32)
-        small = jnp.sum((small * small).reshape(CH // 8, 8, 2 * B), axis=0)
-        hh[...] = hh[...] + both[:, : 2 * B]
-        hl[...] = hl[...] + both[:, 2 * B :]
-        return small
-
-    def gram(get):
+    dims = (((0,), (0,)), ((), ()))
+
+    def gram():
         hh[...] = jnp.zeros_like(hh)
         hl[...] = jnp.zeros_like(hl)
-        small = lax.fori_loop(
-            0, chunks, lambda c, acc: acc + add_gram(get(c), c), jnp.zeros((8, 2 * B), F32)
-        )
+
+        def add(c, acc):
+            load(c).wait()
+            high, low = split(x[at(c), :])
+            both = lax.dot_general(high, jnp.concatenate([high, low], 1), dims, preferred_element_type=F32)
+            small = low.astype(F32)
+            hh[...] = hh[...] + both[:, : 2 * B]
+            hl[...] = hl[...] + both[:, 2 * B :]
+            return acc + jnp.sum((small * small).reshape(CH // 8, 8, 2 * B), axis=0)
+
+        small = lax.fori_loop(0, chunks, add, jnp.zeros((8, 2 * B), F32))
         small = jnp.sum(small, axis=0, keepdims=True)
         rows = lax.broadcasted_iota(jnp.int32, (B, B), 0)
         cols = lax.broadcasted_iota(jnp.int32, (B, B), 1)
@@ -181,59 +203,90 @@
                 block = block + jnp.where(rows == cols, small[:, i * B : (i + 1) * B], 0.0)
             g[pl.ds(place * B, B), :] = block
 
-    def reduce_all(step):
+    def exchange(index, src, dst):
+        copy = remote(src, dst, core_send.at[index], core_recv.at[index], twin)
+        copy.start()
+        copy.wait()
+
+    def share(step, ref, own):
+        copies = []
+        for i, peer in enumerate(peers):
+            copies.append(remote(
+                ref.at[own, :], ref.at[own, :], z_send.at[step, 7 + i], z_recv.at[step, 7 + i], peer
+            ))
+            copies[-1].start()
+        for copy in copies:
+            copy.wait()
+
+    def reduce_all():
         mine = pl.ds(pl.multiple_of(core * 192, 8), 192)
         other = pl.ds(pl.multiple_of((1 - core) * 192, 8), 192)
-        copy = remote(g.at[other, :], half.at[:, :], core_send.at[2 * step], core_recv.at[2 * step], twin)
-        copy.start()
-        copy.wait()
+        own = pl.ds(pl.multiple_of(core * 192 + z * 24, 8), 24)
+        exchange(0, g.at[other, :], half.at[:, :])
         g[mine, :] = g[mine, :] + half[...]
         copies = []
         for i, peer in enumerate(peers):
             rows = pl.ds(pl.multiple_of(core * 192 + (peer[0] // 2) * 24, 8), 24)
-            copies.append(remote(
-                g.at[rows, :], piece.at[step, i], z_send.at[step, i], z_recv.at[step, i], peer
-            ))
+            copies.append(remote(g.at[rows, :], piece.at[i], z_send.at[0, i], z_recv.at[0, i], peer))
             copies[-1].start()
         for copy in copies:
             copy.wait()
-        own = pl.ds(pl.multiple_of(core * 192 + z * 24, 8), 24)
         total = g[own, :]
         for i in range(7):
-            total = total + piece[step, i]
-        done = full.at[step]
-        done[own, :] = total
+            total = total + piece[i]
+        full[own, :] = total
+        share(0, full, own)
+        exchange(1, full.at[mine, :], full.at[mine, :])
+
+    def reduce_cross(started):
+        mine = pl.ds(pl.multiple_of(core * 64, 8), 64)
+        other = pl.ds(pl.multiple_of((1 - core) * 64, 8), 64)
+        own = pl.ds(pl.multiple_of(core * 64 + z * 8, 8), 8)
+        exchange(2, cross.at[:, other, :], cross_half)
+        cross[:, mine, :] = cross[:, mine, :] + cross_half[...]
         copies = []
+        for i, device in enumerate(far):
+            rows = pl.ds(pl.multiple_of(core * 64 + (device[0] // 2) * 8, 8), 8)
+            copies.append(remote(cross.at[1, rows, :], far_piece.at[i], far_send.at[i], far_recv.at[i], device))
+            copies[-1].start()
         for i, peer in enumerate(peers):
-            copies.append(remote(
-                done.at[own, :], done.at[own, :], z_send.at[step, 7 + i], z_recv.at[step, 7 + i], peer
-            ))
+            rows = pl.ds(pl.multiple_of(core * 64 + (peer[0] // 2) * 8, 8), 8)
+            copies.append(remote(cross.at[0, rows, :], own_piece.at[i], z_send.at[1, i], z_recv.at[1, i], peer))
             copies[-1].start()
+        started()
         for copy in copies:
             copy.wait()
-        copy = remote(done.at[mine, :], done.at[mine, :], core_send.at[2 * step + 1], core_recv.at[2 * step + 1], twin)
-        copy.start()
-        copy.wait()
-
-    def solve(step):
-        reduce_all(step)
-        inner_rounds(counts[step], full.at[step], q, ra, rc, re, rd, ccol, scol)
+        total = cross[0, own, :] + far_piece[0]
+        for i in range(7):
+            total = total + (own_piece[i] + far_piece[i + 1])
+        cross_full[own, :] = total
+        share(1, cross_full, own)
+        exchange(3, cross_full.at[mine, :], cross_full.at[mine, :])
+
+    def arrange(step):
         left = jnp.full((8, B), flags[step, 0], jnp.int32) == 1
         for k in range(32):
             qa, qb = q[tile(k), 0:B], q[tile(k), B : 2 * B]
             q[tile(k), 0:B] = jnp.where(left, qb, qa)
             q[tile(k), B : 2 * B] = jnp.where(left, qa, qb)
-        qhi[...], qlo[...] = split(q[...])
+        qhi[...], rest = split_rest(q[...])
+        qmid[...], rest = split_rest(rest)
+        qlo[...] = rest.astype(BF16)
+        return left
 
     def multiply(block):
         high, low = split(block)
         qh = qhi[...]
-        out = jnp.dot(low, qh, preferred_element_type=F32)
-        out = out + jnp.dot(high, qlo[...], preferred_element_type=F32)
+        out = jnp.dot(high, qlo[...], preferred_element_type=F32)
+        out = out + jnp.dot(low, qh, preferred_element_type=F32)
+        out = out + jnp.dot(high, qmid[...], preferred_element_type=F32)
         return out + jnp.dot(high, qh, preferred_element_type=F32)
 
     def t_copy(c):
         return remote(t.at[at(c), :], tin.at[at(c), :], t_send.at[c], t_recv.at[c], fwd)
+
+    def s_copy(c):
+        return remote(s.at[at(c), :], sin.at[at(c - mid), :], s_send.at[c - mid], s_recv.at[c - mid], bwd)
 
     def u_copy(c):
         return remote(u.at[at(c), :], out_hbm.at[at(c), B : 2 * B], u_send.at[c], u_recv.at[c], fwd)
@@ -243,21 +296,37 @@
             return remote(w1.at[:, B : 2 * B], w1in, w_send.at[0], w_recv.at[0], fwd)
         return remote(w2.at[:, B : 2 * B], w2in, w_send.at[1], w_recv.at[1], fwd)
 
-    def loaded(c):
-        load(c).wait()
-        return x[at(c), :]
-
-    gram(loaded)
-    solve(0)
-
-    def first_step(c, _):
+    d_copy = remote(d_out, d_in, d_send.at[0], d_recv.at[0], fwd)
+
+    gram()
+    pl.semaphore_wait(barrier, 17)
+    reduce_all()
+    for k in range(16):
+        ra[tile(k), :] = full[spaced(k), :]
+        rd[tile(k), :] = full[spaced(k, 2 * B), :]
+    surplus = inner_rounds(counts[0], full.at[pl.ds(B, B), :], q, ra, rc, re, rd, ccol, scol)
+    left = arrange(0)
+
+    def rotate(c):
         y = multiply(x[at(c), :])
         s[at(c), :] = y[:, :B]
         t[at(c), :] = y[:, B:]
-        t_copy(c).start()
+
+    def first_step(i, _):
+        rotate(i)
+        t_copy(i).start()
+        rotate(mid + i)
+        s_copy(mid + i).start()
         return 0
 
-    lax.fori_loop(0, chunks, first_step, 0)
+    lax.fori_loop(0, mid, first_step, 0)
+
+    for k, second in enumerate(undo_moves(rd, surplus)):
+        first = ra[tile(k), :]
+        ra[tile(k), :] = jnp.where(left, second, first)
+        d_out[tile(k), :] = jnp.where(left, first, second)
+    d_copy.start()
+
     @pl.when(owner)
     def _():
         w1[...] = q[...]
@@ -271,28 +340,53 @@
     def _():
         w1in[...] = jnp.zeros_like(w1in)
 
-    def pair(c):
-        return jnp.concatenate([s[at(c), :], tin[at(c), :]], 1)
-
-    def arrived(c):
-        t_copy(c).wait_recv()
-        return pair(c)
-
-    gram(arrived)
-    solve(1)
+    hh[...] = jnp.zeros_like(hh)
+    hl[...] = jnp.zeros_like(hl)
+
+    def inner(one, two):
+        one, two = jnp.concatenate(split(one), 1), jnp.concatenate(split(two), 1)
+        return lax.dot_general(one, two, dims, preferred_element_type=F32)
+
+    def meet(i, _):
+        t_copy(i).wait_recv()
+        hh[...] = hh[...] + inner(s[at(i), :], tin[at(i), :])
+        s_copy(mid + i).wait_recv()
+        hl[...] = hl[...] + inner(sin[at(i), :], t[at(mid + i), :])
+        return 0
+
+    lax.fori_loop(0, mid, meet, 0)
+    for place, ref in enumerate((hh, hl)):
+        mixed = ref[:B, B:] + ref[B:, :B]
+        cross[place] = ref[:B, :B] + (mixed + ref[B:, B:])
+
+    def send_rest():
+        lax.fori_loop(mid, chunks, lambda c, _: (t_copy(c).start(), 0)[1], 0)
+
+    reduce_cross(send_rest)
+    d_copy.wait()
+    for k in range(16):
+        rd[tile(k), :] = d_in[tile(k), :]
+    inner_rounds(counts[1], cross_full, q, ra, rc, re, rd, ccol, scol)
+    arrange(1)
 
     def stay_copy(c):
-        return pltpu.make_async_copy(s.at[at(c), :], out_hbm.at[at(c), 0:B], store_sem.at[c])
+        return pltpu.make_async_copy(v.at[at(c), :], out_hbm.at[at(c), 0:B], store_sem.at[c])
 
     def second_step(c, _):
-        y = multiply(pair(c))
+        y = multiply(jnp.concatenate([s[at(c), :], tin[at(c), :]], 1))
         u[at(c), :] = y[:, B:]
         u_copy(c).start()
-        s[at(c), :] = y[:, :B]
+        v[at(c), :] = y[:, :B]
         stay_copy(c).start()
         return 0
 
-    lax.fori_loop(0, chunks, second_step, 0)
+    lax.fori_loop(0, mid, second_step, 0)
+
+    def rest_of_second_step(c, _):
+        t_copy(c).wait_recv()
+        return second_step(c, _)
+
+    lax.fori_loop(mid, chunks, rest_of_second_step, 0)
 
     @pl.when(next_owner)
     def _():
@@ -317,6 +411,7 @@
         return 0
 
     lax.fori_loop(0, chunks, finish, 0)
+    lax.fori_loop(mid, chunks, lambda c, _: (s_copy(c).wait_send(), 0)[1], 0)
 
     @pl.when(owner)
     def _():
@@ -342,6 +437,7 @@
     dma = pltpu.SemaphoreType.DMA
     square = pltpu.VMEM((B, B), F32)
     wide = pltpu.VMEM((2 * B, 2 * B), F32)
+    narrow = pltpu.VMEM((2 * B, 2 * B), BF16)
     tall = pltpu.VMEM((2 * B, B), F32)
     column = pltpu.VMEM((rows, B), F32)
     return pl.pallas_call(
@@ -353,14 +449,16 @@
         in_specs=[smem, smem, anywhere],
         out_specs=(anywhere, vmem),
         scratch_shapes=[
-            pltpu.VMEM((rows, 2 * B), F32), column, column, column, column,
-            pltpu.VMEM((3 * B, B), F32), wide, wide, wide,
-            pltpu.VMEM((2 * B, 2 * B), BF16), pltpu.VMEM((2 * B, 2 * B), BF16),
+            pltpu.VMEM((rows, 2 * B), F32), column, column, column, pltpu.VMEM((rows // 2, B), F32), column, column,
+            pltpu.VMEM((3 * B, B), F32), wide, wide, wide, narrow, narrow, narrow,
             square, square, square, square, square, square,
-            pltpu.VMEM((192, B), F32), pltpu.VMEM((2, 7, 24, B), F32), pltpu.VMEM((2, 3 * B, B), F32),
+            pltpu.VMEM((192, B), F32), pltpu.VMEM((7, 24, B), F32), pltpu.VMEM((3 * B, B), F32),
+            pltpu.VMEM((2, B, B), F32), pltpu.VMEM((2, 64, B), F32),
+            pltpu.VMEM((7, 8, B), F32), pltpu.VMEM((8, 8, B), F32), square, square, square,
             wide, tall, wide, tall,
-            dma((chunks,)), dma((chunks,)), dma((chunks,)), dma((chunks,)), dma((chunks,)), dma((chunks,)),
-            dma((4,)), dma((4,)), dma((2, 14)), dma((2, 14)), dma((2,)), dma((2,)),
+            dma((chunks,)), dma((chunks,)), dma((chunks,)), dma((chunks,)),
+            dma((chunks // 2,)), dma((chunks // 2,)), dma((chunks,)), dma((chunks,)),
+            dma((4,)), dma((4,)), dma((2, 14)), dma((2, 14)), dma((8,)), dma((8,)), dma((2,)), dma((2,)), dma((1,)), dma((1,)),
         ],
         compiler_params=pltpu.CompilerParams(
             collective_id=0, has_side_effects=True, vmem_limit_bytes=56 * 2**20

time: 169 us -> 145 us (0.86)
  Pallas kernels: 156 us -> 134 us
    pallas_call x1, Pallas kernels: 156 us -> 134 us  [per_device(): pl.pallas_call(body, out_shape=(jax.ShapeDtypeStruct((rows, 2 * B), F32),...]
where the time goes in v1:
time: 145 us
  Pallas kernels  134 us (92%)
  local copies, waits for them, and re-layouts  6.52 us (4%)
  other arithmetic  3.94 us (3%)
    pallas_call x1, Pallas kernels, per_device(): pl.pallas_call(body, out_shape=(jax.ShapeDtypeStruct((rows, 2 * B), F32),...  134 us
    unnamed x5, local copies, waits for them, and re-layouts  6.52 us
    mul x1, other arithmetic, per_device(): scaled = jacobian * row_weight[:, None] * col_scale[None, :]  3.94 us

profile of v1, /device:TPU:1, one launch (start us, length us, event | category | flops | bytes accessed | tf_op | source)
XLA Modules:
  0.0 145.1 jit_solution(6848993591796657511)
XLA Ops:
  0.6 1.3 copy.7.flags
  1.9 3.9 %multiply_multiply_fusion.x_hbm = f32[4096,256]{1,0:T(8,128)} fusion(f32[4096,256]{1,0:T(8,128)} %param.5, f32[256]{0:T(256)} %param.7, f32[4096]{0:T(1024)} %param.6), kind=kLoop, calls=%fused_computation | loop fusion | flops 2097152 | bytes 8406016 | tf_op jit(solution)/shard_map/mul | solution.py:431
  5.9 134.0 %jacobi.1 = (f32[4096,256]{1,0:T(8,128)}, f32[256,256]{1,0:T(8,128)}) custom-call(s32[2]{0:T(128)} %counts.1, s32[2,1]{1,0:T(2,128)} %copy.7.flags, f32[4096,256]{1,0:T(8,128)} %multiply_multiply_fusion.x_hbm), custom_call_target="tpu_custom_call" | custom-call | tf_op jit(solution)/shard_map/jacobi/pallas_call | solution.py:443
  139.9 0.0 copy-start
  139.9 4.5 %copy.10 = f32[4096,256]{1,0:T(8,128)} copy(f32[4096,256]{1,0:T(8,128)} %get-tuple-element.4) | data formatting | bytes 8388608
  144.4 0.0 copy-done
  144.4 0.7 copy.11
Async XLA Ops:
  139.9 4.5 %copy-start = (f32[256,256]{1,0:T(8,128)S(1)}, f32[256,256]{1,0:T(8,128)}, u32[]{:S(2)}) copy-start(f32[256,256]{1,0:T(8,128)} %get-tuple-element.5) | copy-start | bytes 786436

commit v2 on v1

--- a/solution.py
+++ b/solution.py
@@ -1,3 +1,5 @@
+import functools
+
 import jax
 import jax.numpy as jnp
 from jax import lax
@@ -9,6 +11,8 @@
 B = 128
 ROUNDS = 24
 CH = 256
+N_Y = 4
+ROUND = 4
 F32 = jnp.float32
 BF16 = jnp.bfloat16
 
@@ -138,11 +142,11 @@
 
 
 def body(
-    counts, flags, x_hbm, out_hbm, w_out,
-    x, s, t, tin, sin, u, v, g, hh, hl, q, qhi, qmid, qlo, ra, rc, re, rd, ccol, scol,
+    counts, flags, weights_hbm, scales_hbm, x_hbm, out_hbm, w_out,
+    weights, scales, x, s, t, tin, sin, u, v, r1, r2, g, hh, hl, q, qhi, qmid, qlo, ra, rc, re, rd, ccol, scol,
     half, piece, full, cross, cross_half, own_piece, far_piece, cross_full, d_out, d_in, w1, w1in, w2, w2in,
-    load_sem, store_sem, t_send, t_recv, s_send, s_recv, u_send, u_recv,
-    core_send, core_recv, z_send, z_recv, far_send, far_recv, w_send, w_recv, d_send, d_recv,
+    small_sem, load_sem, store_sem, t_send, t_recv, s_send, s_recv, u_send, u_recv,
+    r_send, r_recv, core_send, core_recv, z_send, z_recv, far_send, far_recv, w_send, w_recv, d_send, d_recv,
 ):
     row, blk = lax.axis_index("rows"), lax.axis_index("blk")
     n_blk = lax.axis_size("blk")
@@ -156,6 +160,11 @@
     peers = [(((z + i) % 8) * 2 + core, blk) for i in range(1, 8)]
     far = [(((z + i) % 8) * 2 + core, next_blk) for i in range(8)]
     far_from = [(((z + i) % 8) * 2 + core, last_blk) for i in range(8)]
+    column = blk // N_Y * N_Y
+    below = (row, column + (blk + N_Y - 1) % N_Y)
+    above = (row, column + (blk + 1) % N_Y)
+    last_hop = (row, (column + (blk + 2) % N_Y + 1) % n_blk)
+    last_hop_from = (row, last_blk // N_Y * N_Y + (last_blk + 2) % N_Y)
     owner = row == blk
     next_owner = row == last_blk
     third_owner = row == (blk + n_blk - 2) % n_blk
@@ -166,10 +175,16 @@
     def load(c):
         return pltpu.make_async_copy(x_hbm.at[at(c), :], x.at[at(c), :], load_sem.at[c])
 
+    small_loads = [
+        pltpu.make_async_copy(weights_hbm, weights, small_sem.at[0]),
+        pltpu.make_async_copy(scales_hbm, scales, small_sem.at[1]),
+    ]
+    for copy in small_loads:
+        copy.start()
     lax.fori_loop(0, chunks, lambda c, _: (load(c).start(), 0)[1], 0)
 
     barrier = pltpu.get_barrier_semaphore()
-    for device in [twin, fwd] + peers + far_from:
+    for device in [twin, fwd, above, last_hop_from] + peers + far_from:
         pl.semaphore_signal(barrier, inc=1, device_id=device, device_id_type=MESH)
 
     def remote(src, dst, send, recv, device):
@@ -183,9 +198,24 @@
         hh[...] = jnp.zeros_like(hh)
         hl[...] = jnp.zeros_like(hl)
 
+        for copy in small_loads:
+            copy.wait()
+        ccol[0 : weights.shape[0], :] = weights[...]
+        ccol[weights.shape[0] :, :] = jnp.zeros((B - weights.shape[0], B), F32)
+        scol[...] = jnp.transpose(ccol[...])
+        lanes = lax.broadcasted_iota(jnp.int32, (B, B), 1)
+        scale = jnp.concatenate([scales[0:1, :], scales[1:2, :]], 1)
+
         def add(c, acc):
             load(c).wait()
-            high, low = split(x[at(c), :])
+            parts = []
+            for i in range(CH // B):
+                column = jnp.where(lanes == c * (CH // B) + i, scol[...], 0.0)
+                column = jnp.sum(column, axis=1, keepdims=True)
+                rows = pl.ds(pl.multiple_of(c * CH + i * B, B), B)
+                parts.append(x[rows, :] * column * scale)
+                x[rows, :] = parts[-1]
+            high, low = split(jnp.concatenate(parts, 0))
             both = lax.dot_general(high, jnp.concatenate([high, low], 1), dims, preferred_element_type=F32)
             small = low.astype(F32)
             hh[...] = hh[...] + both[:, : 2 * B]
@@ -264,7 +294,7 @@
         exchange(3, cross_full.at[mine, :], cross_full.at[mine, :])
 
     def arrange(step):
-        left = jnp.full((8, B), flags[step, 0], jnp.int32) == 1
+        left = jnp.full((8, B), flags[0, step], jnp.int32) == 1
         for k in range(32):
             qa, qb = q[tile(k), 0:B], q[tile(k), B : 2 * B]
             q[tile(k), 0:B] = jnp.where(left, qb, qa)
@@ -291,6 +321,13 @@
     def u_copy(c):
         return remote(u.at[at(c), :], out_hbm.at[at(c), B : 2 * B], u_send.at[c], u_recv.at[c], fwd)
 
+    def relay(hop, c):
+        if hop == 0:
+            return remote(u.at[at(c), :], r1.at[at(c), :], r_send.at[0, c], r_recv.at[0, c], below)
+        if hop == 1:
+            return remote(r1.at[at(c), :], r2.at[at(c), :], r_send.at[1, c], r_recv.at[1, c], below)
+        return remote(r2.at[at(c), :], out_hbm.at[at(c), B : 2 * B], r_send.at[2, c], u_recv.at[c], last_hop)
+
     def w_copy(step):
         if step == 0:
             return remote(w1.at[:, B : 2 * B], w1in, w_send.at[0], w_recv.at[0], fwd)
@@ -299,7 +336,7 @@
     d_copy = remote(d_out, d_in, d_send.at[0], d_recv.at[0], fwd)
 
     gram()
-    pl.semaphore_wait(barrier, 17)
+    pl.semaphore_wait(barrier, 19)
     reduce_all()
     for k in range(16):
         ra[tile(k), :] = full[spaced(k), :]
@@ -372,21 +409,29 @@
     def stay_copy(c):
         return pltpu.make_async_copy(v.at[at(c), :], out_hbm.at[at(c), 0:B], store_sem.at[c])
 
-    def second_step(c, _):
+    def second_step(c, send):
         y = multiply(jnp.concatenate([s[at(c), :], tin[at(c), :]], 1))
         u[at(c), :] = y[:, B:]
-        u_copy(c).start()
+        send(c).start()
         v[at(c), :] = y[:, :B]
         stay_copy(c).start()
-        return 0
-
-    lax.fori_loop(0, mid, second_step, 0)
-
-    def rest_of_second_step(c, _):
+
+    def round_step(c, _):
+        second_step(c, functools.partial(relay, 0))
+        return 0
+
+    def near_step(c, _):
+        second_step(c, u_copy)
+        return 0
+
+    def late_step(c, _):
         t_copy(c).wait_recv()
-        return second_step(c, _)
-
-    lax.fori_loop(mid, chunks, rest_of_second_step, 0)
+        second_step(c, u_copy)
+        return 0
+
+    lax.fori_loop(0, ROUND, round_step, 0)
+    lax.fori_loop(ROUND, mid, near_step, 0)
+    lax.fori_loop(mid, chunks, late_step, 0)
 
     @pl.when(next_owner)
     def _():
@@ -403,9 +448,25 @@
     def _():
         w_out[:, B:] = jnp.zeros((2 * B, B), F32)
 
+    for hop in (0, 1):
+
+        def pass_on(c, _, hop=hop):
+            relay(hop, c).wait_recv()
+            relay(hop + 1, c).start()
+            return 0
+
+        lax.fori_loop(0, ROUND, pass_on, 0)
+
+    def finish_round(c, _):
+        for hop in range(3):
+            relay(hop, c).wait_send()
+        return 0
+
+    lax.fori_loop(0, ROUND, finish_round, 0)
+    lax.fori_loop(ROUND, chunks, lambda c, _: (u_copy(c).wait_send(), 0)[1], 0)
+
     def finish(c, _):
         t_copy(c).wait_send()
-        u_copy(c).wait_send()
         u_copy(c).wait_recv()
         stay_copy(c).wait()
         return 0
@@ -428,11 +489,11 @@
 
 
 def per_device(jacobian, row_weight, col_scale, round_count, move_flag):
-    scaled = jacobian * row_weight[:, None] * col_scale[None, :]
-    rows = scaled.shape[0]
+    rows = jacobian.shape[0]
     chunks = rows // CH
     anywhere = pl.BlockSpec(memory_space=pl.ANY)
     vmem = pl.BlockSpec(memory_space=pltpu.VMEM)
+    hbm = pl.BlockSpec(memory_space=pltpu.HBM)
     smem = pl.BlockSpec(memory_space=pltpu.SMEM)
     dma = pltpu.SemaphoreType.DMA
     square = pltpu.VMEM((B, B), F32)
@@ -440,31 +501,34 @@
     narrow = pltpu.VMEM((2 * B, 2 * B), BF16)
     tall = pltpu.VMEM((2 * B, B), F32)
     column = pltpu.VMEM((rows, B), F32)
+    relayed = pltpu.VMEM((ROUND * CH, B), F32)
     return pl.pallas_call(
         body,
         out_shape=(
             jax.ShapeDtypeStruct((rows, 2 * B), F32),
             jax.ShapeDtypeStruct((2 * B, 2 * B), F32),
         ),
-        in_specs=[smem, smem, anywhere],
+        in_specs=[smem, smem, hbm, hbm, hbm],
         out_specs=(anywhere, vmem),
         scratch_shapes=[
+            pltpu.VMEM((rows // B, B), F32), pltpu.VMEM((2, B), F32),
             pltpu.VMEM((rows, 2 * B), F32), column, column, column, pltpu.VMEM((rows // 2, B), F32), column, column,
+            relayed, relayed,
             pltpu.VMEM((3 * B, B), F32), wide, wide, wide, narrow, narrow, narrow,
             square, square, square, square, square, square,
             pltpu.VMEM((192, B), F32), pltpu.VMEM((7, 24, B), F32), pltpu.VMEM((3 * B, B), F32),
             pltpu.VMEM((2, B, B), F32), pltpu.VMEM((2, 64, B), F32),
             pltpu.VMEM((7, 8, B), F32), pltpu.VMEM((8, 8, B), F32), square, square, square,
             wide, tall, wide, tall,
-            dma((chunks,)), dma((chunks,)), dma((chunks,)), dma((chunks,)),
+            dma((2,)), dma((chunks,)), dma((chunks,)), dma((chunks,)), dma((chunks,)),
             dma((chunks // 2,)), dma((chunks // 2,)), dma((chunks,)), dma((chunks,)),
-            dma((4,)), dma((4,)), dma((2, 14)), dma((2, 14)), dma((8,)), dma((8,)), dma((2,)), dma((2,)), dma((1,)), dma((1,)),
+            dma((3, ROUND)), dma((2, ROUND)), dma((4,)), dma((4,)), dma((2, 14)), dma((2, 14)), dma((8,)), dma((8,)), dma((2,)), dma((2,)), dma((1,)), dma((1,)),
         ],
         compiler_params=pltpu.CompilerParams(
             collective_id=0, has_side_effects=True, vmem_limit_bytes=56 * 2**20
         ),
         name="jacobi",
-    )(round_count, move_flag, scaled)
+    )(round_count, move_flag.T, row_weight.reshape(rows // B, B), col_scale.reshape(2, B), jacobian)
 
 
 def solution(mesh):

time: 145 us -> 131 us (0.903)
  Pallas kernels: 134 us -> 125 us
  other arithmetic: 3.94 us -> 0 us
    pallas_call x1, Pallas kernels: 134 us -> 125 us  [per_device(): pl.pallas_call(body, out_shape=(jax.ShapeDtypeStruct((rows, 2 * B), F32),...]
    mul x1 -> x0, other arithmetic: 3.94 us -> none  [per_device(): scaled = jacobian * row_weight[:, None] * col_scale[None, :]]
    unnamed x5 -> x4, local copies, waits for them, and re-layouts: 6.52 us -> 5.22 us
where the time goes in v2:
time: 131 us
  Pallas kernels  125 us (95%)
  local copies, waits for them, and re-layouts  5.22 us (4%)
    pallas_call x1, Pallas kernels, per_device(): pl.pallas_call(body, out_shape=(jax.ShapeDtypeStruct((rows, 2 * B), F32),...  125 us
    unnamed x4, local copies, waits for them, and re-layouts  5.22 us

profile of v2, /device:TPU:1, one launch (start us, length us, event | category | flops | bytes accessed | tf_op | source)
XLA Modules:
  0.0 130.6 jit_solution(6377777149172695410)
XLA Ops:
  0.6 124.7 %jacobi.1 = (f32[4096,256]{1,0:T(8,128)}, f32[256,256]{1,0:T(8,128)}) custom-call(s32[2]{0:T(128)} %counts.1, s32[1,2]{1,0:T(1,128)} %bitcast.5, f32[32,128]{1,0:T(8,128)} %bitcast.3, f32[2,128]{1,0:T(2,128)} %bitcast.4, f32[4096,256]{1,0:T(8,128)} %x_hbm.1), custom_call_target="tpu_custom_call" | custom-call | tf_op jit(solution)/shard_map/jacobi/pallas_call | solution.py:505
  125.4 0.0 copy-start
  125.4 4.5 %copy.9 = f32[4096,256]{1,0:T(8,128)} copy(f32[4096,256]{1,0:T(8,128)} %get-tuple-element.4) | data formatting | bytes 8388608
  129.9 0.0 copy-done
  129.9 0.7 copy.10
Async XLA Ops:
  125.4 4.5 %copy-start = (f32[256,256]{1,0:T(8,128)S(1)}, f32[256,256]{1,0:T(8,128)}, u32[]{:S(2)}) copy-start(f32[256,256]{1,0:T(8,128)} %get-tuple-element.5) | copy-start | bytes 786436

commit v3 on v2

--- a/solution.py
+++ b/solution.py
@@ -12,7 +12,9 @@
 ROUNDS = 24
 CH = 256
 N_Y = 4
-ROUND = 4
+ROUND = 3
+AHEAD = 4
+EARLY = 4
 F32 = jnp.float32
 BF16 = jnp.bfloat16
 
@@ -29,12 +31,11 @@
 
 def rotation(first, second, cross, live):
     diff = second - first
-    radius = jnp.sqrt(diff * diff + 4.0 * cross * cross)
-    signs = jnp.where(diff >= 0.0, 1.0, -1.0)
-    tangent = signs * 2.0 * cross / (jnp.abs(diff) + radius)
-    cosine = 1.0 / jnp.sqrt(1.0 + tangent * tangent)
-    sine = cosine * tangent
-    return jnp.where(live, cosine, 1.0), jnp.where(live, sine, 0.0)
+    inverse = lax.rsqrt(diff * diff + 4.0 * cross * cross)
+    square = 0.5 + 0.5 * (jnp.abs(diff) * inverse)
+    scale = lax.rsqrt(square)
+    sine = jnp.where(diff >= 0.0, cross, -cross) * inverse * scale
+    return jnp.where(live, square * scale, 1.0), jnp.where(live, sine, 0.0)
 
 
 def tile(k):
@@ -45,47 +46,67 @@
     return pl.ds(start + k, 8, stride=16)
 
 
-def inner_rounds(count, cross, q, a, c, e, d, ccol, scol):
+def inner_rounds(count, cross, out, q, upper, lower, a, c, e, d, ccol, scol):
     count = jnp.full((8, B), count, jnp.int32)
     lane = lax.broadcasted_iota(jnp.int32, (8, B), 1)
     sub = lax.broadcasted_iota(jnp.int32, (8, B), 0)
-    low = lane % 16
-    on_diag = (lane // 16) == sub
-    nxt = (lane + (B - 1)) % B
-    nlow = nxt % 16
-    on_next = (nxt // 16) == sub
-    ccol[...] = jnp.transpose(cross[...])
+
+    def band(distance):
+        row = (lane + (B - distance)) % B
+        return row % 16, (row // 16) == sub
+
+    bands = [band(distance) for distance in range(3)]
+
+    def left(x, distance=1):
+        return pltpu.roll(x, B - distance, 1)
+
+    def total(x, distance):
+        x = jnp.where(bands[distance][1], x, 0.0)
+        return jnp.broadcast_to(jnp.sum(x, axis=0, keepdims=True), (8, B))
+
+    def pick(ref, distance):
+        acc = jnp.zeros((8, B), F32)
+        for k in range(16):
+            acc = jnp.where(bands[distance][0] == k, ref[tile(k), :], acc)
+        return left(total(acc, distance), distance) if distance else total(acc, 0)
+
+    def spread(cs, sn, place):
+        for k in range(16):
+            own = bands[0][1] & (bands[0][0] == k)
+            ccol[place, tile(k), :] = jnp.broadcast_to(jnp.sum(jnp.where(own, cs, 0.0), axis=1, keepdims=True), (8, B))
+            scol[place, tile(k), :] = jnp.broadcast_to(jnp.sum(jnp.where(own, sn, 0.0), axis=1, keepdims=True), (8, B))
+
+    ccol[0] = jnp.transpose(cross[...])
     for k in range(16):
         c[tile(k), :] = cross[spaced(k), :]
-        e[tile(k), :] = ccol[spaced(k), :]
-    rows = lax.broadcasted_iota(jnp.int32, (2 * B, 2 * B), 0)
-    cols = lax.broadcasted_iota(jnp.int32, (2 * B, 2 * B), 1)
-    q[...] = (rows == cols).astype(F32)
-
-    def pick(ref):
-        acc = jnp.zeros((8, B), F32)
-        for k in range(16):
-            acc = jnp.where(low == k, ref[tile(k), :], acc)
-        return total(jnp.where(on_diag, acc, 0.0))
-
-    def total(x):
-        return jnp.broadcast_to(jnp.sum(x, axis=0, keepdims=True), (8, B))
-
-    def spread(cs, sn):
-        ccol[...] = jnp.transpose(jnp.broadcast_to(cs[0:1], (B, B)))
-        scol[...] = jnp.transpose(jnp.broadcast_to(sn[0:1], (B, B)))
-
-    cs, sn = rotation(pick(a), pick(d), pick(c), 0 < count)
-    spread(cs, sn)
-
-    def one(index, carry):
-        cs, sn = carry
-        acc_a = acc_c = acc_d = jnp.zeros((8, B), F32)
+        e[tile(k), :] = ccol[0, spaced(k), :]
+    wide_lane = lax.broadcasted_iota(jnp.int32, (8, 2 * B), 1)
+    wide_row = 16 * lax.broadcasted_iota(jnp.int32, (8, 2 * B), 0)
+    for k in range(16):
+        upper[tile(k), :] = (wide_lane == wide_row + k).astype(F32)
+        lower[tile(k), :] = (wide_lane == wide_row + (B + k)).astype(F32)
+    diag_a, diag_d, diag_c = pick(a, 0), pick(d, 0), pick(c, 0)
+    near = pick(a, 1), pick(c, 1), pick(e, 1), pick(d, 1)
+    cs, sn = rotation(diag_a, diag_d, diag_c, 0 < count)
+    spread(cs, sn, 0)
+
+    def one(index, place, carry):
+        cs, sn, diag_a, diag_d, diag_c, near_a, near_c, near_e, near_d = carry
+        new_c = left(sn) * (cs * near_a - sn * near_e) + left(cs) * (cs * near_c - sn * near_d)
+        new_a = cs * (cs * diag_a - sn * diag_c) - sn * (cs * diag_c - sn * diag_d)
+        new_d = left(sn * (sn * diag_a + cs * diag_c) + cs * (sn * diag_c + cs * diag_d))
+        new = rotation(new_a, new_d, new_c, index + 1 < count)
+        spread(*new, 1 - place)
+        acc_a = acc_c = acc_d = acc_e = jnp.zeros((8, B), F32)
         first = None
         for k in range(16):
             before = tile((k - 1) % 16)
-            ck, sk = ccol[spaced(k), :], scol[spaced(k), :]
+            ck, sk = ccol[place, tile(k), :], scol[place, tile(k), :]
             ak, bk, ek, dk = a[tile(k), :], c[tile(k), :], e[tile(k), :], d[tile(k), :]
+            cw, sw = jnp.concatenate([ck, ck], 1), jnp.concatenate([sk, sk], 1)
+            qu, ql = upper[tile(k), :], lower[tile(k), :]
+            upper[tile(k), :] = cw * qu - sw * ql
+            q2 = sw * qu + cw * ql
             a1 = ck * ak - sk * ek
             e1 = sk * ak + ck * ek
             b1 = ck * bk - sk * dk
@@ -94,39 +115,52 @@
             b2 = a1 * sn + b1 * cs
             e2 = e1 * cs - d1 * sn
             d2 = e1 * sn + d1 * cs
-            acc_a = jnp.where(low == k, a2, acc_a)
-            acc_d = jnp.where(low == k, d2, acc_d)
-            acc_c = jnp.where(nlow == k, b2, acc_c)
+            acc_a = jnp.where(bands[1][0] == k, a2, acc_a)
+            acc_c = jnp.where(bands[2][0] == k, b2, acc_c)
+            acc_e = jnp.where(bands[0][0] == k, e2, acc_e)
+            acc_d = jnp.where(bands[1][0] == k, d2, acc_d)
             a[tile(k), :] = a2
-            c[tile(k), :] = pltpu.roll(b2, B - 1, 1)
-            d3 = pltpu.roll(d2, B - 1, 1)
+            c[tile(k), :] = left(b2)
+            d3 = left(d2)
             if k == 0:
-                first = (e2, d3)
+                first = (e2, d3, q2)
             else:
+                lower[before, :] = q2
                 e[before, :] = e2
                 d[before, :] = d3
         e[tile(15), :] = pltpu.roll(first[0], 7, 0)
         d[tile(15), :] = pltpu.roll(first[1], 7, 0)
-        diag_a = total(jnp.where(on_diag, acc_a, 0.0))
-        diag_d = pltpu.roll(total(jnp.where(on_diag, acc_d, 0.0)), B - 1, 1)
-        diag_c = pltpu.roll(total(jnp.where(on_next, acc_c, 0.0)), B - 1, 1)
-        new = rotation(diag_a, diag_d, diag_c, index + 1 < count)
-        for k in range(32):
-            qa, qb = q[tile(k), 0:B], q[tile(k), B : 2 * B]
-            q[tile(k), 0:B] = qa * cs - qb * sn
-            q[tile(k), B : 2 * B] = pltpu.roll(qa * sn + qb * cs, B - 1, 1)
-        spread(*new)
-        return new
-
-    lax.fori_loop(0, ROUNDS, one, (cs, sn))
+        lower[tile(15), :] = pltpu.roll(first[2], 7, 0)
+        near = (left(total(acc_a, 1)), left(total(acc_c, 2), 2), left(total(acc_e, 0)), left(total(acc_d, 1), 2))
+        return (*new, new_a, new_d, new_c, *near)
+
+    def two(index, carry):
+        return one(2 * index + 1, 1, one(2 * index, 0, carry))
+
+    lax.fori_loop(0, ROUNDS // 2, two, (cs, sn, diag_a, diag_d, diag_c, *near))
     extra = ROUNDS - count
     surplus = [(extra >> bit) % 2 == 1 for bit in range(5)]
-    for k in range(32):
-        qb = q[tile(k), B : 2 * B]
-        for bit in range(5):
-            qb = jnp.where(surplus[bit], pltpu.roll(qb, 1 << bit, 1), qb)
-        q[tile(k), B : 2 * B] = qb
+    tiles = [lower[tile(k), :] for k in range(16)]
+    for bit in range(5):
+        tiles = undo_rows(tiles, bit, surplus[bit])
+    for k in range(16):
+        q[spaced(k), :] = tiles[k][:, :B]
+        q[spaced(k, B), :] = tiles[k][:, B:]
+    out[:B, B:], out[B:, B:] = jnp.transpose(q[:B, :]), jnp.transpose(q[B:, :])
+    for k in range(16):
+        q[spaced(k), :] = upper[tile(k), :B]
+        q[spaced(k, B), :] = upper[tile(k), B:]
+    out[:B, :B], out[B:, :B] = jnp.transpose(q[:B, :]), jnp.transpose(q[B:, :])
     return surplus
+
+
+def undo_rows(tiles, bit, on):
+    move = 1 << bit
+    moved = []
+    for k in range(16):
+        value = tiles[(k - move) % 16]
+        moved.append(value if k >= move else pltpu.roll(value, 1, 0))
+    return [jnp.where(on[0:1, 0:1], new, old) for new, old in zip(moved, tiles)]
 
 
 def undo_moves(d, surplus):
@@ -143,16 +177,19 @@
 
 def body(
     counts, flags, weights_hbm, scales_hbm, x_hbm, out_hbm, w_out,
-    weights, scales, x, s, t, tin, sin, u, v, r1, r2, g, hh, hl, q, qhi, qmid, qlo, ra, rc, re, rd, ccol, scol,
+    x_in, s_in, t_far, q_in0, q_in1, p0a, p0b, p0c, p1a, p1b, p1c,
+    x_send, x_recv, f_send, f_recv, q_send, q_recv, far_sem,
+    weights, scales, x, s, t, tin, sin, u, v, r1, r2, g, hh, hl, q, qn, qa, qb, qhi, qmid, qlo, ra, rc, re, rd, ccol, scol,
     half, piece, full, cross, cross_half, own_piece, far_piece, cross_full, d_out, d_in, w1, w1in, w2, w2in,
     small_sem, load_sem, store_sem, t_send, t_recv, s_send, s_recv, u_send, u_recv,
     r_send, r_recv, core_send, core_recv, z_send, z_recv, far_send, far_recv, w_send, w_recv, d_send, d_recv,
 ):
+    q_in, q_parts = (q_in0, q_in1), ((p0a, p0b, p0c), (p1a, p1b, p1c))
     row, blk = lax.axis_index("rows"), lax.axis_index("blk")
     n_blk = lax.axis_size("blk")
     z, core = row // 2, row % 2
     chunks = x.shape[0] // CH
-    mid = chunks // 2
+    mid = (AHEAD + chunks) // 2
     next_blk = (blk + 1) % n_blk
     last_blk = (blk + n_blk - 1) % n_blk
     fwd, bwd = (row, next_blk), (row, last_blk)
@@ -187,6 +224,8 @@
     for device in [twin, fwd, above, last_hop_from] + peers + far_from:
         pl.semaphore_signal(barrier, inc=1, device_id=device, device_id_type=MESH)
 
+    pl.semaphore_wait(barrier, 19)
+
     def remote(src, dst, send, recv, device):
         return pltpu.make_async_remote_copy(
             src_ref=src, dst_ref=dst, send_sem=send, recv_sem=recv, device_id=device, device_id_type=MESH
@@ -200,21 +239,23 @@
 
         for copy in small_loads:
             copy.wait()
-        ccol[0 : weights.shape[0], :] = weights[...]
-        ccol[weights.shape[0] :, :] = jnp.zeros((B - weights.shape[0], B), F32)
-        scol[...] = jnp.transpose(ccol[...])
+        ccol[0, 0 : weights.shape[0], :] = weights[...]
+        ccol[0, weights.shape[0] :, :] = jnp.zeros((B - weights.shape[0], B), F32)
+        scol[0] = jnp.transpose(ccol[0])
         lanes = lax.broadcasted_iota(jnp.int32, (B, B), 1)
         scale = jnp.concatenate([scales[0:1, :], scales[1:2, :]], 1)
 
-        def add(c, acc):
+        def add(ahead, c, acc):
             load(c).wait()
             parts = []
             for i in range(CH // B):
-                column = jnp.where(lanes == c * (CH // B) + i, scol[...], 0.0)
+                column = jnp.where(lanes == c * (CH // B) + i, scol[0], 0.0)
                 column = jnp.sum(column, axis=1, keepdims=True)
                 rows = pl.ds(pl.multiple_of(c * CH + i * B, B), B)
                 parts.append(x[rows, :] * column * scale)
                 x[rows, :] = parts[-1]
+            if ahead:
+                x_copy(c).start()
             high, low = split(jnp.concatenate(parts, 0))
             both = lax.dot_general(high, jnp.concatenate([high, low], 1), dims, preferred_element_type=F32)
             small = low.astype(F32)
@@ -222,7 +263,8 @@
             hl[...] = hl[...] + both[:, 2 * B :]
             return acc + jnp.sum((small * small).reshape(CH // 8, 8, 2 * B), axis=0)
 
-        small = lax.fori_loop(0, chunks, add, jnp.zeros((8, 2 * B), F32))
+        small = lax.fori_loop(0, EARLY, functools.partial(add, True), jnp.zeros((8, 2 * B), F32))
+        small = lax.fori_loop(EARLY, chunks, functools.partial(add, False), small)
         small = jnp.sum(small, axis=0, keepdims=True)
         rows = lax.broadcasted_iota(jnp.int32, (B, B), 0)
         cols = lax.broadcasted_iota(jnp.int32, (B, B), 1)
@@ -238,14 +280,17 @@
         copy.start()
         copy.wait()
 
-    def share(step, ref, own):
+    def share_start(step, ref, own):
         copies = []
         for i, peer in enumerate(peers):
             copies.append(remote(
                 ref.at[own, :], ref.at[own, :], z_send.at[step, 7 + i], z_recv.at[step, 7 + i], peer
             ))
             copies[-1].start()
-        for copy in copies:
+        return copies
+
+    def share(step, ref, own):
+        for copy in share_start(step, ref, own):
             copy.wait()
 
     def reduce_all():
@@ -299,17 +344,50 @@
             qa, qb = q[tile(k), 0:B], q[tile(k), B : 2 * B]
             q[tile(k), 0:B] = jnp.where(left, qb, qa)
             q[tile(k), B : 2 * B] = jnp.where(left, qa, qb)
-        qhi[...], rest = split_rest(q[...])
-        qmid[...], rest = split_rest(rest)
-        qlo[...] = rest.astype(BF16)
+        three(q, qhi, qmid, qlo)
         return left
 
-    def multiply(block):
+    def three(source, high, middle, low):
+        high[...], rest = split_rest(source[...])
+        middle[...], rest = split_rest(rest)
+        low[...] = rest.astype(BF16)
+
+    def q_copy(step):
+        own = pl.ds(pl.multiple_of(core * B + z * 16, 16), 16)
+        source = q.at[own, :] if step == 0 else q.at[own, B : 2 * B]
+        return remote(source, q_in[step].at[own, :], q_send.at[step], q_recv.at[step], fwd)
+
+    def gather_begin(step):
+        own = pl.ds(pl.multiple_of(core * B + z * 16, 16), 16)
+        q_copy(step).wait()
+        return share_start(2 + step, q_in[step], own)
+
+    def gather_middle(step, copies):
+        mine = pl.ds(pl.multiple_of(core * B, B), B)
+        for copy in copies:
+            copy.wait()
+        last = remote(
+            q_in[step].at[mine, :], q_in[step].at[mine, :], core_send.at[4 + step], core_recv.at[4 + step], twin
+        )
+        last.start()
+        return last
+
+    def gather_end(step, last):
+        last.wait()
+        three(q_in[step], *q_parts[step])
+
+    def x_copy(c):
+        return remote(x.at[at(c), :], x_in.at[at(c), :], x_send.at[c], x_recv.at[c], fwd)
+
+    def far_copy(c):
+        return remote(tin.at[at(c), :], t_far.at[at(c), :], f_send.at[c], f_recv.at[c], fwd)
+
+    def multiply(block, parts=(qhi, qmid, qlo)):
         high, low = split(block)
-        qh = qhi[...]
-        out = jnp.dot(high, qlo[...], preferred_element_type=F32)
+        qh = parts[0][...]
+        out = jnp.dot(high, parts[2][...], preferred_element_type=F32)
         out = out + jnp.dot(low, qh, preferred_element_type=F32)
-        out = out + jnp.dot(high, qmid[...], preferred_element_type=F32)
+        out = out + jnp.dot(high, parts[1][...], preferred_element_type=F32)
         return out + jnp.dot(high, qh, preferred_element_type=F32)
 
     def t_copy(c):
@@ -322,11 +400,12 @@
         return remote(u.at[at(c), :], out_hbm.at[at(c), B : 2 * B], u_send.at[c], u_recv.at[c], fwd)
 
     def relay(hop, c):
+        i = c - AHEAD
         if hop == 0:
-            return remote(u.at[at(c), :], r1.at[at(c), :], r_send.at[0, c], r_recv.at[0, c], below)
+            return remote(u.at[at(c), :], r1.at[at(i), :], r_send.at[0, i], r_recv.at[0, i], below)
         if hop == 1:
-            return remote(r1.at[at(c), :], r2.at[at(c), :], r_send.at[1, c], r_recv.at[1, c], below)
-        return remote(r2.at[at(c), :], out_hbm.at[at(c), B : 2 * B], r_send.at[2, c], u_recv.at[c], last_hop)
+            return remote(r1.at[at(i), :], r2.at[at(i), :], r_send.at[1, i], r_recv.at[1, i], below)
+        return remote(r2.at[at(i), :], out_hbm.at[at(c), B : 2 * B], r_send.at[2, i], u_recv.at[c], last_hop)
 
     def w_copy(step):
         if step == 0:
@@ -336,12 +415,12 @@
     d_copy = remote(d_out, d_in, d_send.at[0], d_recv.at[0], fwd)
 
     gram()
-    pl.semaphore_wait(barrier, 19)
     reduce_all()
+    lax.fori_loop(EARLY, AHEAD, lambda c, _: (x_copy(c).start(), 0)[1], 0)
     for k in range(16):
         ra[tile(k), :] = full[spaced(k), :]
         rd[tile(k), :] = full[spaced(k, 2 * B), :]
-    surplus = inner_rounds(counts[0], full.at[pl.ds(B, B), :], q, ra, rc, re, rd, ccol, scol)
+    surplus = inner_rounds(counts[0], full.at[pl.ds(B, B), :], q, qn, qa, qb, ra, rc, re, rd, ccol, scol)
     left = arrange(0)
 
     def rotate(c):
@@ -350,13 +429,20 @@
         t[at(c), :] = y[:, B:]
 
     def first_step(i, _):
-        rotate(i)
-        t_copy(i).start()
+        rotate(AHEAD + i)
+        t_copy(AHEAD + i).start()
         rotate(mid + i)
         s_copy(mid + i).start()
         return 0
 
-    lax.fori_loop(0, mid, first_step, 0)
+    q_copy(0).start()
+    lax.fori_loop(0, mid - AHEAD, first_step, 0)
+
+    def rotate_own(c, _):
+        s[at(c), :] = multiply(x[at(c), :])[:, :B]
+        return 0
+
+    lax.fori_loop(0, AHEAD, rotate_own, 0)
 
     for k, second in enumerate(undo_moves(rd, surplus)):
         first = ra[tile(k), :]
@@ -384,27 +470,46 @@
         one, two = jnp.concatenate(split(one), 1), jnp.concatenate(split(two), 1)
         return lax.dot_general(one, two, dims, preferred_element_type=F32)
 
+    pending = gather_begin(0)
+
+    def meet_own(c, _):
+        x_copy(c).wait_recv()
+        y = multiply(x_in[at(c), :], q_parts[0])
+        s_in[at(c), :] = y[:, :B]
+        tin[at(c), :] = y[:, B:]
+        hh[...] = hh[...] + inner(s[at(c), :], y[:, B:])
+        return 0
+
     def meet(i, _):
-        t_copy(i).wait_recv()
-        hh[...] = hh[...] + inner(s[at(i), :], tin[at(i), :])
+        c = AHEAD + i
+        t_copy(c).wait_recv()
+        hh[...] = hh[...] + inner(s[at(c), :], tin[at(c), :])
         s_copy(mid + i).wait_recv()
         hl[...] = hl[...] + inner(sin[at(i), :], t[at(mid + i), :])
         return 0
 
-    lax.fori_loop(0, mid, meet, 0)
+    pairs = mid - AHEAD
+    lax.fori_loop(0, pairs // 3, meet, 0)
+    pending = gather_middle(0, pending)
+    lax.fori_loop(pairs // 3, pairs * 2 // 3, meet, 0)
+    gather_end(0, pending)
+    lax.fori_loop(0, AHEAD, meet_own, 0)
+    lax.fori_loop(pairs * 2 // 3, pairs, meet, 0)
     for place, ref in enumerate((hh, hl)):
         mixed = ref[:B, B:] + ref[B:, :B]
         cross[place] = ref[:B, :B] + (mixed + ref[B:, B:])
 
     def send_rest():
         lax.fori_loop(mid, chunks, lambda c, _: (t_copy(c).start(), 0)[1], 0)
+        lax.fori_loop(0, AHEAD, lambda c, _: (far_copy(c).start(), 0)[1], 0)
 
     reduce_cross(send_rest)
     d_copy.wait()
     for k in range(16):
         rd[tile(k), :] = d_in[tile(k), :]
-    inner_rounds(counts[1], cross_full, q, ra, rc, re, rd, ccol, scol)
+    inner_rounds(counts[1], cross_full, q, qn, qa, qb, ra, rc, re, rd, ccol, scol)
     arrange(1)
+    q_copy(1).start()
 
     def stay_copy(c):
         return pltpu.make_async_copy(v.at[at(c), :], out_hbm.at[at(c), 0:B], store_sem.at[c])
@@ -429,9 +534,26 @@
         second_step(c, u_copy)
         return 0
 
-    lax.fori_loop(0, ROUND, round_step, 0)
-    lax.fori_loop(ROUND, mid, near_step, 0)
+    def own_step(c, _):
+        y = multiply(jnp.concatenate([s[at(c), :], tin[at(c), :]], 1))
+        v[at(c), :] = y[:, :B]
+        stay_copy(c).start()
+        return 0
+
+    def far_store(c):
+        return pltpu.make_async_copy(u.at[at(c), :], out_hbm.at[at(c), B : 2 * B], far_sem.at[c])
+
+    def far_step(c, _):
+        far_copy(c).wait_recv()
+        u[at(c), :] = multiply(jnp.concatenate([s_in[at(c), :], t_far[at(c), :]], 1), q_parts[1])
+        far_store(c).start()
+        return 0
+
+    lax.fori_loop(AHEAD, AHEAD + ROUND, round_step, 0)
+    lax.fori_loop(AHEAD + ROUND, mid, near_step, 0)
     lax.fori_loop(mid, chunks, late_step, 0)
+    lax.fori_loop(0, AHEAD, own_step, 0)
+    pending = gather_begin(1)
 
     @pl.when(next_owner)
     def _():
@@ -455,15 +577,20 @@
             relay(hop + 1, c).start()
             return 0
 
-        lax.fori_loop(0, ROUND, pass_on, 0)
+        lax.fori_loop(AHEAD, AHEAD + ROUND, pass_on, 0)
+        if hop == 0:
+            pending = gather_middle(1, pending)
+
+    gather_end(1, pending)
+    lax.fori_loop(0, AHEAD, far_step, 0)
 
     def finish_round(c, _):
         for hop in range(3):
             relay(hop, c).wait_send()
         return 0
 
-    lax.fori_loop(0, ROUND, finish_round, 0)
-    lax.fori_loop(ROUND, chunks, lambda c, _: (u_copy(c).wait_send(), 0)[1], 0)
+    lax.fori_loop(AHEAD, AHEAD + ROUND, finish_round, 0)
+    lax.fori_loop(AHEAD + ROUND, chunks, lambda c, _: (u_copy(c).wait_send(), 0)[1], 0)
 
     def finish(c, _):
         t_copy(c).wait_send()
@@ -471,7 +598,15 @@
         stay_copy(c).wait()
         return 0
 
-    lax.fori_loop(0, chunks, finish, 0)
+    def finish_own(c, _):
+        x_copy(c).wait_send()
+        far_copy(c).wait_send()
+        far_store(c).wait()
+        stay_copy(c).wait()
+        return 0
+
+    lax.fori_loop(AHEAD, chunks, finish, 0)
+    lax.fori_loop(0, AHEAD, finish_own, 0)
     lax.fori_loop(mid, chunks, lambda c, _: (s_copy(c).wait_send(), 0)[1], 0)
 
     @pl.when(owner)
@@ -497,10 +632,14 @@
     smem = pl.BlockSpec(memory_space=pltpu.SMEM)
     dma = pltpu.SemaphoreType.DMA
     square = pltpu.VMEM((B, B), F32)
+    double = pltpu.VMEM((2, B, B), F32)
     wide = pltpu.VMEM((2 * B, 2 * B), F32)
     narrow = pltpu.VMEM((2 * B, 2 * B), BF16)
     tall = pltpu.VMEM((2 * B, B), F32)
+    flat = pltpu.VMEM((B, 2 * B), F32)
     column = pltpu.VMEM((rows, B), F32)
+    ahead = pltpu.VMEM((AHEAD * CH, B), F32)
+    thin = pltpu.VMEM((2 * B, B), BF16)
     relayed = pltpu.VMEM((ROUND * CH, B), F32)
     return pl.pallas_call(
         body,
@@ -511,18 +650,21 @@
         in_specs=[smem, smem, hbm, hbm, hbm],
         out_specs=(anywhere, vmem),
         scratch_shapes=[
+            pltpu.VMEM((AHEAD * CH, 2 * B), F32), ahead, ahead, wide, tall,
+            narrow, narrow, narrow, thin, thin, thin,
+            dma((AHEAD,)), dma((AHEAD,)), dma((AHEAD,)), dma((AHEAD,)), dma((2,)), dma((2,)), dma((AHEAD,)),
             pltpu.VMEM((rows // B, B), F32), pltpu.VMEM((2, B), F32),
             pltpu.VMEM((rows, 2 * B), F32), column, column, column, pltpu.VMEM((rows // 2, B), F32), column, column,
             relayed, relayed,
-            pltpu.VMEM((3 * B, B), F32), wide, wide, wide, narrow, narrow, narrow,
-            square, square, square, square, square, square,
+            pltpu.VMEM((3 * B, B), F32), wide, wide, wide, tall, flat, flat, narrow, narrow, narrow,
+            square, square, square, square, double, double,
             pltpu.VMEM((192, B), F32), pltpu.VMEM((7, 24, B), F32), pltpu.VMEM((3 * B, B), F32),
             pltpu.VMEM((2, B, B), F32), pltpu.VMEM((2, 64, B), F32),
             pltpu.VMEM((7, 8, B), F32), pltpu.VMEM((8, 8, B), F32), square, square, square,
             wide, tall, wide, tall,
             dma((2,)), dma((chunks,)), dma((chunks,)), dma((chunks,)), dma((chunks,)),
             dma((chunks // 2,)), dma((chunks // 2,)), dma((chunks,)), dma((chunks,)),
-            dma((3, ROUND)), dma((2, ROUND)), dma((4,)), dma((4,)), dma((2, 14)), dma((2, 14)), dma((8,)), dma((8,)), dma((2,)), dma((2,)), dma((1,)), dma((1,)),
+            dma((3, ROUND)), dma((2, ROUND)), dma((6,)), dma((6,)), dma((4, 14)), dma((4, 14)), dma((8,)), dma((8,)), dma((2,)), dma((2,)), dma((1,)), dma((1,)),
         ],
         compiler_params=pltpu.CompilerParams(
             collective_id=0, has_side_effects=True, vmem_limit_bytes=56 * 2**20

time: 131 us -> 126 us (0.962)
  Pallas kernels: 125 us -> 120 us
    pallas_call x1, Pallas kernels: 125 us -> 120 us  [per_device(): pl.pallas_call(body, out_shape=(jax.ShapeDtypeStruct((rows, 2 * B), F32),...]
where the time goes in v3:
time: 126 us
  Pallas kernels  120 us (95%)
  local copies, waits for them, and re-layouts  5.22 us (4%)
    pallas_call x1, Pallas kernels, per_device(): pl.pallas_call(body, out_shape=(jax.ShapeDtypeStruct((rows, 2 * B), F32),...  120 us
    unnamed x4, local copies, waits for them, and re-layouts  5.22 us

profile of v3, /device:TPU:1, one launch (start us, length us, event | category | flops | bytes accessed | tf_op | source)
XLA Modules:
  0.0 126.2 jit_solution(14939722367425460363)
XLA Ops:
  0.6 120.4 %jacobi.1 = (f32[4096,256]{1,0:T(8,128)}, f32[256,256]{1,0:T(8,128)}) custom-call(s32[2]{0:T(128)} %counts.1, s32[1,2]{1,0:T(1,128)} %bitcast.5, f32[32,128]{1,0:T(8,128)} %bitcast.3, f32[2,128]{1,0:T(2,128)} %bitcast.4, f32[4096,256]{1,0:T(8,128)} %x_hbm.1), custom_call_target="tpu_custom_call" | custom-call | tf_op jit(solution)/shard_map/jacobi/pallas_call | solution.py:644
  121.0 0.0 copy-start
  121.0 4.5 %copy.9 = f32[4096,256]{1,0:T(8,128)} copy(f32[4096,256]{1,0:T(8,128)} %get-tuple-element.4) | data formatting | bytes 8388608
  125.5 0.0 copy-done
  125.5 0.7 copy.10
Async XLA Ops:
  121.0 4.5 %copy-start = (f32[256,256]{1,0:T(8,128)S(1)}, f32[256,256]{1,0:T(8,128)}, u32[]{:S(2)}) copy-start(f32[256,256]{1,0:T(8,128)} %get-tuple-element.5) | copy-start | bytes 786436

commit v4 on v3

--- a/solution.py
+++ b/solution.py
@@ -667,7 +667,7 @@
             dma((3, ROUND)), dma((2, ROUND)), dma((6,)), dma((6,)), dma((4, 14)), dma((4, 14)), dma((8,)), dma((8,)), dma((2,)), dma((2,)), dma((1,)), dma((1,)),
         ],
         compiler_params=pltpu.CompilerParams(
-            collective_id=0, has_side_effects=True, vmem_limit_bytes=56 * 2**20
+            collective_id=0, has_side_effects=True, vmem_limit_bytes=46 * 2**20
         ),
         name="jacobi",
     )(round_count, move_flag.T, row_weight.reshape(rows // B, B), col_scale.reshape(2, B), jacobian)

time: 126 us -> 126 us (level)
    unnamed x4 -> x10, local copies, waits for them, and re-layouts: 5.22 us -> 5.42 us
where the time goes in v4:
time: 126 us; the launch traced here: 125 us
  Pallas kernels  119 us (94%)
  local copies, waits for them, and re-layouts  5.42 us (4%)
    pallas_call x1, Pallas kernels, per_device(): pl.pallas_call(body, out_shape=(jax.ShapeDtypeStruct((rows, 2 * B), F32),...  119 us
    unnamed x10, local copies, waits for them, and re-layouts  5.42 us

profile of v4, /device:TPU:1, one launch (start us, length us, event | category | flops | bytes accessed | tf_op | source)
XLA Modules:
  0.0 125.4 jit_solution(14664391839153487118)
XLA Ops:
  0.6 0.0 copy-start
  0.6 0.7 copy-done
  1.3 0.0 copy-start.1
  1.4 0.7 copy-done.1
  2.0 0.0 copy-start.2
  2.0 0.7 copy-done.2
  2.7 0.0 copy-start.3
  2.7 0.7 copy-done.3
  3.3 119.3 %jacobi.1 = (f32[4096,256]{1,0:T(8,128)S(1)}, f32[256,256]{1,0:T(8,128)S(1)}) custom-call(s32[2]{0:T(128)S(1)} %copy-done.2, s32[1,2]{1,0:T(1,128)S(1)} %bitcast.5, f32[32,128]{1,0:T(8,128)S(1)} %bitcast.3, f32[2,128]{1,0:T(2,128)S(1)} %bitcast.4, f32[4096,256]{1,0:T(8,128)} %x_hbm.1), custom_call_target="tpu_custom_call" | custom-call | tf_op jit(solution)/shard_map/jacobi/pallas_call | solution.py:644
  122.6 2.0 %copy.9 = f32[4096,256]{1,0:T(8,128)} copy(f32[4096,256]{1,0:T(8,128)S(1)} %get-tuple-element.4) | data formatting | bytes 8388608
  124.7 0.7 copy.10
Async XLA Ops:
  0.6 0.7 copy-start
  1.3 0.7 copy-start.1
  2.0 0.7 copy-start.2
  2.7 0.7 copy-start.3
